TPU v7x, 256 devices: a whole 4x4x8 slice. The times are simulated.
256 devices in a mesh: oct: 8 (over x, core), box: 32 (over y, z).
Axes of the slice: x: 4, y: 4, z: 8, core: 2. Of those that a mesh axis runs over, the one named last changes fastest.
Arguments:
- multipole6: float32 [121, 32768], P(None, ('oct', 'box')), may hold values from -21 to 21
- local5: float32 [121, 4096], P(None, ('oct', 'box')), may hold values from -6 to 6
- box_ids: int32 [4096], P(('oct', 'box')), may hold values from 0 to 32767, as said below
- box_count: int32 [256], P(('oct', 'box')), may hold values from 1 to 16, as said below
- up_shift: float32 [8, 121, 121], replicated, may hold values from -0.5 to 0.5
- down_shift: float32 [8, 121, 121], replicated, may hold values from -0.5 to 0.5
- periodic_lattice_operator: float32 [121, 121], replicated, may hold values from -0.0029296875 to 0.0029296875
- multipole_to_wave_maps: float32 [6, 256, 121], replicated, may hold values from -0.5 to 0.5
- wave_to_local_maps: float32 [6, 121, 256], replicated, may hold values from -0.0625 to 0.0625
- wave_shift: float32 [6, 36, 256], replicated, may hold values from 0.02 to 1
- local_source: int32 [6, 256, 2048], P(None, ('oct', 'box')), may hold values from 0 to 127, as said below
- local_target: int32 [6, 256, 2048], P(None, ('oct', 'box')), may hold values from 0 to 127, as said below
- local_class: int32 [6, 256, 2048], P(None, ('oct', 'box')), may hold values from 0 to 35
- remote_source: int32 [6, 256, 8, 64], P(None, ('oct', 'box')), may hold values from 0 to 127, as said below
- remote_class: int32 [6, 256, 8, 64], P(None, ('oct', 'box')), may hold values from 0 to 35
- remote_count: int32 [6, 256, 8], P(None, ('oct', 'box')), may hold values from 0 to 64, as said below
- arrival_slot: int32 [6, 256, 8, 64], P(None, ('oct', 'box')), may hold values from 0 to 127, as said below
Outputs:
- local6: float32 [121, 32768], P(None, ('oct', 'box'))
Inputs may be any that keep to these rules, and one draw needn't show every extreme that they name: `box_count`: 16 is reached by some device in every draw. `box_ids`: device q holds consecutive Morton ids in its slots, starting at q * 128 plus an offset, in slots below its count; slots beyond hold 0; the first device starts at 0 and the last device's range ends at the last id. `local_source`: a slot of a box that device q holds, below 8 box_count[q]. `local_target`: a slot of a box that device q holds, below 8 box_count[q]; every entry is valid. `remote_source`: a slot of a box that the sender holds, below 8 times its count. `remote_count`: in each direction some receiver gets exactly 64 entries from each of its 8 neighbours. `arrival_slot`: a slot of a box that the receiver holds, below 8 times its count; entries at or past the count carry nothing.
All inputs are finite; a program needn't handle non-finite values.
Results may differ from a plain program's by a relative error of at most 0.0003.
Values sent between devices are 32-bit elements; how exact they have to be, the bound alone decides.
A program may use at most 128 MiB of HBM per device.

v0:
```python
import functools

import jax
import jax.numpy as jnp
from jax import lax
from jax.experimental import pallas as pl
from jax.experimental.pallas import tpu as pltpu
from jax.sharding import PartitionSpec as P

K = 121
KP = 128
NEXP = 256
CLASSES = 36
DEPTH = 5
NEIGH = 8
BOX5 = 16
CAP = 64
LOC = 2048
SLOTS = 128
BLOCKS = LOC // 128
DIRS = 6
OFFSETS = [(n // 2 + 1) * (1 if n % 2 == 0 else -1) for n in range(NEIGH)]
MESH = pl.DeviceIdType.MESH
F32 = jnp.float32
BF16 = jnp.bfloat16


def split(x):
    hi = x.astype(BF16)
    return hi, (x - hi.astype(F32)).astype(BF16)


def mm(a, b):
    return jnp.dot(a, b, preferred_element_type=F32)


def mm_nt(a, b):
    return lax.dot_general(a, b, (((1,), (1,)), ((), ())), preferred_element_type=F32)


def mm3(a, b):
    ah, al = split(a)
    bh, bl = split(b)
    return mm(ah, bh) + (mm(ah, bl) + mm(al, bh))


def pick_lanes(table, index):
    index = jnp.broadcast_to(index, table.shape)
    numbers = lax.GatherDimensionNumbers(
        offset_dims=(),
        collapsed_slice_dims=(1,),
        start_index_map=(1,),
        operand_batching_dims=(0,),
        start_indices_batching_dims=(0,),
    )
    return lax.gather(
        table,
        index[..., None],
        numbers,
        slice_sizes=(1, 1),
        mode=lax.GatherScatterMode.PROMISE_IN_BOUNDS,
    )


def lane_iota(rows):
    return lax.broadcasted_iota(jnp.int32, (rows, 128), 1)


def one_hot_rows(index):
    rows = lax.broadcasted_iota(jnp.int32, (128, 128), 0)
    return jnp.where(rows == index, 1.0, 0.0).astype(BF16)


def shift_level(high_ref, low_ref, fields, digits):
    fh, fl = split(fields)
    total = jnp.zeros((KP, 128), F32)
    for c in range(8):
        mask = jnp.where(digits == c, 1.0, 0.0).astype(BF16)
        ch, cl = fh * mask, fl * mask
        total = total + (mm(high_ref[c], ch) + (mm(high_ref[c], cl) + mm(low_ref[c], ch)))
    return total


def scatter_block(rows, target):
    hi, lo = split(rows)
    hot = one_hot_rows(target)
    return mm_nt(jnp.concatenate([hi, lo], axis=1), jnp.concatenate([hot, hot], axis=1))


def kernel(
    comm,
    multipole_ref,
    local5_ref,
    ids_ref,
    count_ref,
    up_ref,
    down_ref,
    lattice_ref,
    to_wave_ref,
    to_local_ref,
    shift_ref,
    near_source_ref,
    near_target_ref,
    near_class_ref,
    far_source_ref,
    far_class_ref,
    far_count_ref,
    arrival_ref,
    out_ref,
    moments,
    far_moments,
    pack,
    far_pack,
    padded,
    up_high,
    up_low,
    down_high,
    down_low,
    expansion,
    factor,
    sums,
    ring_a,
    ring_b,
    far_send,
    far_recv,
    pack_send,
    pack_recv,
    a_send,
    a_recv,
    b_send,
    b_recv,
):
    if comm:
        octant, box = lax.axis_index("oct"), lax.axis_index("box")
        flat = octant * 32 + box
        x, core = lax.div(octant, 2), lax.rem(octant, 2)
        y, z = lax.div(box, 8), lax.rem(box, 8)

        def neighbour(offset):
            other = lax.rem(flat + offset + 256, 256)
            return lax.div(other, 32), lax.rem(other, 32)

        def peer_a(k):
            rank = lax.rem(core * 8 + z + k, 16)
            return x * 2 + lax.div(rank, 8), y * 8 + lax.rem(rank, 8)

        def peer_b(k):
            rank = lax.rem(x * 4 + y + k, 16)
            return lax.div(rank, 4) * 2 + core, lax.rem(rank, 4) * 8 + z

        barrier = pltpu.get_barrier_semaphore()
        for n in range(NEIGH):
            pl.semaphore_signal(barrier, inc=1, device_id=neighbour(OFFSETS[n]), device_id_type=MESH)

        def greet(k, carry):
            pl.semaphore_signal(barrier, inc=1, device_id=peer_a(k), device_id_type=MESH)
            pl.semaphore_signal(barrier, inc=1, device_id=peer_b(k), device_id_type=MESH)
            return carry

        lax.fori_loop(1, 16, greet, 0)

    lanes = lane_iota(1)
    count = count_ref[0]
    valid = jnp.where(lanes < 8 * count, 1.0, 0.0)

    moments[...] = jnp.zeros((KP, 128), F32)
    moments[:K, :] = multipole_ref[...] * valid

    wide_lane = lax.broadcasted_iota(jnp.int32, (NEIGH, CAP), 1)
    row_number = lax.broadcasted_iota(jnp.int32, (NEIGH, CAP), 0)
    for d in range(DIRS):
        limit = jnp.zeros((NEIGH, CAP), jnp.int32)
        for n in range(NEIGH):
            limit = jnp.where(row_number == n, far_count_ref[d, 0, n], limit)
        source = jnp.where(wide_lane < limit, far_source_ref[d], -1)
        pack[:, d, :] = jnp.concatenate([source, far_class_ref[d]], axis=1)

    padded[...] = jnp.zeros((KP, KP), F32)
    for c in range(8):
        padded[:K, :K] = up_ref[:, c, :]
        up_high[c], up_low[c] = split(padded[...])
        padded[:K, :K] = down_ref[:, c, :]
        down_high[c], down_low[c] = split(padded[...])

    ids = jnp.concatenate([ids_ref[...], jnp.zeros((1, 128 - BOX5), jnp.int32)], axis=1)
    parent_of = lane_iota(8) // 8
    ids = pick_lanes(jnp.broadcast_to(ids, (8, 128)), parent_of[:1])[:1]
    child = lanes % 8
    digit = [(ids >> (3 * (DEPTH - j))) & 7 for j in range(1, DEPTH + 1)]

    upward = shift_level(up_high, up_low, moments[...], child)
    for j in range(DEPTH - 1, -1, -1):
        upward = shift_level(up_high, up_low, upward, digit[j])
    upward = upward * valid
    ring_a[0] = jnp.sum(jnp.transpose(upward), axis=0, keepdims=True)

    if comm:
        pl.semaphore_wait(barrier, NEIGH + 15 + 15)

        def far_copies(n):
            who = neighbour(OFFSETS[n])
            return (
                pltpu.make_async_remote_copy(
                    src_ref=moments,
                    dst_ref=far_moments.at[n],
                    send_sem=far_send.at[n],
                    recv_sem=far_recv.at[n],
                    device_id=who,
                    device_id_type=MESH,
                ),
                pltpu.make_async_remote_copy(
                    src_ref=pack.at[n],
                    dst_ref=far_pack.at[n],
                    send_sem=pack_send.at[n],
                    recv_sem=pack_recv.at[n],
                    device_id=who,
                    device_id_type=MESH,
                ),
            )

        def sum_copy(k, ring, send, recv, peer):
            return pltpu.make_async_remote_copy(
                src_ref=ring.at[0],
                dst_ref=ring.at[k],
                send_sem=send.at[k - 1],
                recv_sem=recv.at[k - 1],
                device_id=peer(k),
                device_id_type=MESH,
            )

        def for_peers(action):
            def body(k, carry):
                action(k)
                return carry

            lax.fori_loop(1, 16, body, 0)

        copy_a = lambda k: sum_copy(k, ring_a, a_send, a_recv, peer_a)
        copy_b = lambda k: sum_copy(k, ring_b, b_send, b_recv, peer_b)
        for_peers(lambda k: copy_a(k).start())
        far = [far_copies(n) for n in range(NEIGH)]
        for pair in far:
            for copy in pair:
                copy.start()
    else:
        for n in range(NEIGH):
            far_moments[n] = moments[...]
            far_pack[n] = pack[n]

    def near_direction(d, carry):
        weight = to_wave_ref[d]
        mh, ml = split(moments[:K, :])
        wh, wl = split(weight)
        expansion[...] = mm(wh, mh) + (mm(wh, ml) + mm(wl, mh))
        table = jnp.concatenate([shift_ref[d], jnp.zeros((128 - CLASSES, NEXP), F32)], axis=0)
        factor[d] = jnp.transpose(table)
        total = jnp.zeros((NEXP, 128), F32)
        for block in range(BLOCKS):
            source = near_source_ref[d, pl.ds(block, 1), :]
            klass = near_class_ref[d, pl.ds(block, 1), :]
            target = near_target_ref[d, pl.ds(block, 1), :]
            rows = pick_lanes(expansion[...], source) * pick_lanes(factor[d], klass)
            total = total + scatter_block(rows, target)
        sums[d] = total
        return carry

    lax.fori_loop(0, DIRS // 2, near_direction, 0)

    if comm:
        for_peers(lambda k: copy_a(k).wait())
        ring_b[0] = jnp.sum(ring_a[...], axis=0)
        for_peers(lambda k: copy_b(k).start())
    else:
        ring_b[0] = ring_a[0]

    lax.fori_loop(DIRS // 2, DIRS, near_direction, 0)

    if comm:
        for_peers(lambda k: copy_b(k).wait())
        root = jnp.sum(ring_b[...], axis=0)
    else:
        root = ring_b[0]

    padded[:K, :K] = lattice_ref[...]
    ah, al = split(padded[...])
    rh, rl = split(jnp.broadcast_to(root, (128, KP)))
    downward = mm_nt(ah, rh) + (mm_nt(ah, rl) + mm_nt(al, rh))
    for j in range(DEPTH):
        downward = shift_level(down_high, down_low, downward, digit[j])
    padded[...] = jnp.zeros((KP, KP), F32)
    padded[:BOX5, :K] = local5_ref[...]
    coarse = pick_lanes(jnp.transpose(padded[...]), parent_of[:1]) + downward
    result = shift_level(down_high, down_low, coarse, child)[:K]

    if comm:
        for pair in far:
            for copy in pair:
                copy.wait()

    first_half = lanes < CAP

    def far_direction(d, result):
        wh, wl = split(to_wave_ref[d])
        total = sums[d]
        arrival = jnp.concatenate([arrival_ref[d], arrival_ref[d]], axis=1)
        for p in range(NEIGH // 2):
            one = far_pack[2 * p, pl.ds(d, 1), :]
            two = far_pack[2 * p + 1, pl.ds(d, 1), :]
            source = jnp.where(first_half, one, pltpu.roll(two, CAP, 1))
            klass = jnp.where(first_half, pltpu.roll(one, CAP, 1), two)
            target = jnp.where(first_half, arrival[2 * p : 2 * p + 1], arrival[2 * p + 1 : 2 * p + 2])
            target = jnp.where(source >= 0, target, -1)
            source = jnp.maximum(source, 0)
            picked = jnp.where(
                first_half,
                pick_lanes(far_moments[2 * p], source),
                pick_lanes(far_moments[2 * p + 1], source),
            )[:K]
            ph, pl_ = split(picked)
            rows = mm(wh, ph) + (mm(wh, pl_) + mm(wl, ph))
            rows = rows * pick_lanes(factor[d], klass)
            total = total + scatter_block(rows, target)
        return result + mm3(to_local_ref[d], total)

    result = lax.fori_loop(0, DIRS, far_direction, result)
    out_ref[...] = result * valid


def local(
    multipole6,
    local5,
    box_ids,
    box_count,
    up_shift,
    down_shift,
    periodic_lattice_operator,
    multipole_to_wave_maps,
    wave_to_local_maps,
    wave_shift,
    local_source,
    local_target,
    local_class,
    remote_source,
    remote_class,
    remote_count,
    arrival_slot,
    comm=True,
):
    vmem = pl.BlockSpec(memory_space=pltpu.VMEM)
    smem = pl.BlockSpec(memory_space=pltpu.SMEM)
    dma = pltpu.SemaphoreType.DMA
    return pl.pallas_call(
        functools.partial(kernel, comm),
        out_shape=jax.ShapeDtypeStruct((K, SLOTS), F32),
        in_specs=[vmem] * 3 + [smem] + [vmem] * 11 + [smem] + [vmem],
        out_specs=vmem,
        scratch_shapes=[
            pltpu.VMEM((KP, 128), F32),
            pltpu.VMEM((NEIGH, KP, 128), F32),
            pltpu.VMEM((NEIGH, 8, 128), jnp.int32),
            pltpu.VMEM((NEIGH, 8, 128), jnp.int32),
            pltpu.VMEM((KP, KP), F32),
            pltpu.VMEM((8, KP, KP), BF16),
            pltpu.VMEM((8, KP, KP), BF16),
            pltpu.VMEM((8, KP, KP), BF16),
            pltpu.VMEM((8, KP, KP), BF16),
            pltpu.VMEM((NEXP, 128), F32),
            pltpu.VMEM((DIRS, NEXP, 128), F32),
            pltpu.VMEM((DIRS, NEXP, 128), F32),
            pltpu.VMEM((16, 1, 128), F32),
            pltpu.VMEM((16, 1, 128), F32),
            dma((NEIGH,)),
            dma((NEIGH,)),
            dma((NEIGH,)),
            dma((NEIGH,)),
            dma((15,)),
            dma((15,)),
            dma((15,)),
            dma((15,)),
        ],
        compiler_params=pltpu.CompilerParams(
            vmem_limit_bytes=40 * 1024 * 1024,
            **(dict(collective_id=0, has_side_effects=True) if comm else {}),
        ),
        name="downward_pass",
    )(
        multipole6,
        jnp.transpose(local5),
        box_ids.reshape(1, BOX5),
        box_count,
        jnp.transpose(up_shift, (1, 0, 2)),
        jnp.transpose(down_shift, (1, 0, 2)),
        periodic_lattice_operator,
        multipole_to_wave_maps,
        wave_to_local_maps,
        wave_shift,
        local_source.reshape(DIRS, BLOCKS, 128),
        local_target.reshape(DIRS, BLOCKS, 128),
        local_class.reshape(DIRS, BLOCKS, 128),
        remote_source.reshape(DIRS, NEIGH, CAP),
        remote_class.reshape(DIRS, NEIGH, CAP),
        remote_count,
        arrival_slot.reshape(DIRS, NEIGH, CAP),
    )


def solution(mesh):
    split_axes = ("oct", "box")
    return jax.shard_map(
        local,
        mesh=mesh,
        in_specs=(
            P(None, split_axes),
            P(None, split_axes),
            P(split_axes),
            P(split_axes),
            P(),
            P(),
            P(),
            P(),
            P(),
            P(),
            P(None, split_axes, None),
            P(None, split_axes, None),
            P(None, split_axes, None),
            P(None, split_axes, None, None),
            P(None, split_axes, None, None),
            P(None, split_axes, None),
            P(None, split_axes, None, None),
        ),
        out_specs=P(None, split_axes),
        check_vma=False,
    )
```

profile of v0, /device:TPU:33, one launch (start us, length us, event | category | flops | bytes accessed | tf_op | source)
XLA Modules:
  0.0 49.9 jit_solution(15677408953611078791)
XLA Ops:
  0.7 0.0 copy-start.13
  0.7 0.0 copy-start.14
  0.7 0.0 copy-start.15
  0.7 0.7 %copy-done.13 = f32[121,16]{0,1:T(8,128)S(1)} copy-done((f32[121,16]{0,1:T(8,128)S(1)}, f32[121,16]{0,1:T(8,128)}, u32[]{:S(2)}) %copy-start.13) | copy-done | bytes 7768
  1.4 0.0 copy-done.14
  1.4 0.0 copy-done.15
  1.4 0.0 copy-start
  1.4 1.1 %copy-done = f32[6,256,121]{2,1,0:T(8,128)S(1)} copy-done((f32[6,256,121]{2,1,0:T(8,128)S(1)}, f32[6,256,121]{2,1,0:T(8,128)}, u32[]{:S(2)}) %copy-start) | copy-done | bytes 743448
  2.5 0.0 copy-start.1
  2.5 1.1 %copy-done.1 = f32[6,121,256]{2,1,0:T(8,128)S(1)} copy-done((f32[6,121,256]{2,1,0:T(8,128)S(1)}, f32[6,121,256]{2,1,0:T(8,128)}, u32[]{:S(2)}) %copy-start.1) | copy-done | bytes 743448
  3.6 0.0 copy-start.2
  3.6 1.0 %copy-done.2 = f32[8,121,121]{2,0,1:T(8,128)S(1)} copy-done((f32[8,121,121]{2,0,1:T(8,128)S(1)}, f32[8,121,121]{2,0,1:T(8,128)}, u32[]{:S(2)}) %copy-start.2) | copy-done | bytes 468536
  4.7 1.0 %copy-done.3 = f32[8,121,121]{2,0,1:T(8,128)S(1)} copy-done((f32[8,121,121]{2,0,1:T(8,128)S(1)}, f32[8,121,121]{2,0,1:T(8,128)}, u32[]{:S(2)}) %copy-start.3) | copy-done | bytes 468536
  5.7 0.9 %copy-done.4 = f32[6,36,256]{2,1,0:T(8,128)S(1)} copy-done((f32[6,36,256]{2,1,0:T(8,128)S(1)}, f32[6,36,256]{2,1,0:T(8,128)}, u32[]{:S(2)}) %copy-start.4) | copy-done | bytes 221208
  6.6 0.8 %copy-done.5 = f32[121,128]{1,0:T(8,128)S(1)} copy-done((f32[121,128]{1,0:T(8,128)S(1)}, f32[121,128]{1,0:T(8,128)}, u32[]{:S(2)}) %copy-start.5) | copy-done | bytes 61976
  7.5 0.8 %copy-done.6 = f32[121,121]{1,0:T(8,128)S(1)} copy-done((f32[121,121]{1,0:T(8,128)S(1)}, f32[121,121]{1,0:T(8,128)}, u32[]{:S(2)}) %copy-start.6) | copy-done | bytes 58588
  8.3 0.8 %copy-done.7 = s32[6,1,2048]{2,1,0:T(1,128)S(1)} copy-done((s32[6,1,2048]{2,1,0:T(1,128)S(1)}, s32[6,1,2048]{2,1,0:T(1,128)}, u32[]{:S(2)}) %copy-start.7) | copy-done | bytes 49176
  9.1 0.8 %copy-done.8 = s32[6,1,2048]{2,1,0:T(1,128)S(1)} copy-done((s32[6,1,2048]{2,1,0:T(1,128)S(1)}, s32[6,1,2048]{2,1,0:T(1,128)}, u32[]{:S(2)}) %copy-start.8) | copy-done | bytes 49176
  9.9 0.8 %copy-done.9 = s32[6,1,2048]{2,1,0:T(1,128)S(1)} copy-done((s32[6,1,2048]{2,1,0:T(1,128)S(1)}, s32[6,1,2048]{2,1,0:T(1,128)}, u32[]{:S(2)}) %copy-start.9) | copy-done | bytes 49176
  10.7 0.7 %copy-done.10 = s32[6,1,8,64]{3,2,1,0:T(8,128)S(1)} copy-done((s32[6,1,8,64]{3,2,1,0:T(8,128)S(1)}, s32[6,1,8,64]{3,2,1,0:T(8,128)}, u32[]{:S(2)}) %copy-start.10) | copy-done | bytes 12312
  11.4 0.7 %copy-done.11 = s32[6,1,8,64]{3,2,1,0:T(8,128)S(1)} copy-done((s32[6,1,8,64]{3,2,1,0:T(8,128)S(1)}, s32[6,1,8,64]{3,2,1,0:T(8,128)}, u32[]{:S(2)}) %copy-start.11) | copy-done | bytes 12312
  12.2 0.7 %copy-done.12 = s32[6,1,8,64]{3,2,1,0:T(8,128)S(1)} copy-done((s32[6,1,8,64]{3,2,1,0:T(8,128)S(1)}, s32[6,1,8,64]{3,2,1,0:T(8,128)}, u32[]{:S(2)}) %copy-start.12) | copy-done | bytes 12312
  12.9 36.4 %downward_pass.1 = f32[121,128]{1,0:T(8,128)S(1)} custom-call(f32[121,128]{1,0:T(8,128)S(1)} %copy-done.5, f32[16,121]{1,0:T(8,128)S(1)} %bitcast.18, s32[1,16]{1,0:T(1,128)S(1)} %bitcast.19, s32[1]{0:T(128)S(6)} %copy.19.count_ref, f32[121,8,121]{2,1,0:T(8,128)S(1)} %bitcast.10, f32[121,8,121]{2,1,0:T(8,128)S(1)} %bitcast.11, f32[121,121]{1,0:T(8,128)S(1)} %copy-done.6, ...), custom_call_target="tpu_custom_call" | custom-call | tf_op jit(solution)/shard_map/downward_pass/pallas_call | solution.py:352
  49.3 0.6 %copy.20 = f32[121,128]{1,0:T(8,128)} copy(f32[121,128]{1,0:T(8,128)S(1)} %downward_pass.1) | data formatting | bytes 123904
  (10 shorter events, 0.0 us)
Async XLA Ops:
  0.7 0.7 %copy-start.13 = (f32[121,16]{0,1:T(8,128)S(1)}, f32[121,16]{0,1:T(8,128)}, u32[]{:S(2)}) copy-start(f32[121,16]{0,1:T(8,128)} %param.18) | copy-start | bytes 23236
  0.7 0.7 %copy-start.14 = (s32[6,1,8]{2,1,0:T(1,128)S(1)}, s32[6,1,8]{2,1,0:T(1,128)}, u32[]{:S(2)}) copy-start(s32[6,1,8]{2,1,0:T(1,128)} %far_count_ref.1) | copy-start | bytes 580
  0.7 0.7 %copy-start.15 = (s32[16]{0:T(128)S(1)}, s32[16]{0:T(128)}, u32[]{:S(2)}) copy-start(s32[16]{0:T(128)} %param.19) | copy-start | bytes 196
  1.4 1.1 %copy-start = (f32[6,256,121]{2,1,0:T(8,128)S(1)}, f32[6,256,121]{2,1,0:T(8,128)}, u32[]{:S(2)}) copy-start(f32[6,256,121]{2,1,0:T(8,128)} %to_wave_ref.1) | copy-start | bytes 2230276
  2.5 1.1 %copy-start.1 = (f32[6,121,256]{2,1,0:T(8,128)S(1)}, f32[6,121,256]{2,1,0:T(8,128)}, u32[]{:S(2)}) copy-start(f32[6,121,256]{2,1,0:T(8,128)} %to_local_ref.1) | copy-start | bytes 2230276
  3.6 1.0 %copy-start.2 = (f32[8,121,121]{2,0,1:T(8,128)S(1)}, f32[8,121,121]{2,0,1:T(8,128)}, u32[]{:S(2)}) copy-start(f32[8,121,121]{2,0,1:T(8,128)} %param.21) | copy-start | bytes 1405540
  4.7 1.0 %copy-start.3 = (f32[8,121,121]{2,0,1:T(8,128)S(1)}, f32[8,121,121]{2,0,1:T(8,128)}, u32[]{:S(2)}) copy-start(f32[8,121,121]{2,0,1:T(8,128)} %param.22) | copy-start | bytes 1405540
  5.7 0.9 %copy-start.4 = (f32[6,36,256]{2,1,0:T(8,128)S(1)}, f32[6,36,256]{2,1,0:T(8,128)}, u32[]{:S(2)}) copy-start(f32[6,36,256]{2,1,0:T(8,128)} %shift_ref.1) | copy-start | bytes 663556
  6.6 0.8 %copy-start.5 = (f32[121,128]{1,0:T(8,128)S(1)}, f32[121,128]{1,0:T(8,128)}, u32[]{:S(2)}) copy-start(f32[121,128]{1,0:T(8,128)} %multipole_ref.1) | copy-start | bytes 185860
  7.5 0.8 %copy-start.6 = (f32[121,121]{1,0:T(8,128)S(1)}, f32[121,121]{1,0:T(8,128)}, u32[]{:S(2)}) copy-start(f32[121,121]{1,0:T(8,128)} %lattice_ref.1) | copy-start | bytes 175696
  8.3 0.8 %copy-start.7 = (s32[6,1,2048]{2,1,0:T(1,128)S(1)}, s32[6,1,2048]{2,1,0:T(1,128)}, u32[]{:S(2)}) copy-start(s32[6,1,2048]{2,1,0:T(1,128)} %param.27) | copy-start | bytes 147460
  9.1 0.8 %copy-start.8 = (s32[6,1,2048]{2,1,0:T(1,128)S(1)}, s32[6,1,2048]{2,1,0:T(1,128)}, u32[]{:S(2)}) copy-start(s32[6,1,2048]{2,1,0:T(1,128)} %param.28) | copy-start | bytes 147460
  9.9 0.8 %copy-start.9 = (s32[6,1,2048]{2,1,0:T(1,128)S(1)}, s32[6,1,2048]{2,1,0:T(1,128)}, u32[]{:S(2)}) copy-start(s32[6,1,2048]{2,1,0:T(1,128)} %param.29) | copy-start | bytes 147460
  10.7 0.7 %copy-start.10 = (s32[6,1,8,64]{3,2,1,0:T(8,128)S(1)}, s32[6,1,8,64]{3,2,1,0:T(8,128)}, u32[]{:S(2)}) copy-start(s32[6,1,8,64]{3,2,1,0:T(8,128)} %param.30) | copy-start | bytes 36868
  11.4 0.7 %copy-start.11 = (s32[6,1,8,64]{3,2,1,0:T(8,128)S(1)}, s32[6,1,8,64]{3,2,1,0:T(8,128)}, u32[]{:S(2)}) copy-start(s32[6,1,8,64]{3,2,1,0:T(8,128)} %param.31) | copy-start | bytes 36868
  12.2 0.7 %copy-start.12 = (s32[6,1,8,64]{3,2,1,0:T(8,128)S(1)}, s32[6,1,8,64]{3,2,1,0:T(8,128)}, u32[]{:S(2)}) copy-start(s32[6,1,8,64]{3,2,1,0:T(8,128)} %param.33) | copy-start | bytes 36868
where the time goes:
time: 50.7 us; the launch traced here: 49.9 us
  Pallas kernels  36.4 us (72%)
  local copies, waits for them, and re-layouts  12.9 us (25%)
  between operations  0.7 us (1%)
    pallas_call x1, Pallas kernels, local(): pl.pallas_call(functools.partial(kernel, comm), out_shape=jax.ShapeDtypeS...  36.4 us
    unnamed x33, local copies, waits for them, and re-layouts  12.9 us

commit v1 on v0

--- a/solution.py
+++ b/solution.py
@@ -21,6 +21,44 @@
 DIRS = 6
 OFFSETS = [(n // 2 + 1) * (1 if n % 2 == 0 else -1) for n in range(NEIGH)]
 MESH = pl.DeviceIdType.MESH
+LOADS = (
+    "multipole",
+    "local5",
+    "ids",
+    "count",
+    "up",
+    "down",
+    "lattice",
+    "to_wave",
+    "to_local",
+    "shift",
+    "near_source",
+    "near_target",
+    "near_class",
+    "far_source",
+    "far_class",
+    "far_count",
+    "arrival",
+)
+LOAD_ORDER = (
+    "count",
+    "far_count",
+    "ids",
+    "multipole",
+    "far_source",
+    "far_class",
+    "up",
+    "to_wave",
+    "shift",
+    "near_source",
+    "near_class",
+    "near_target",
+    "down",
+    "lattice",
+    "local5",
+    "arrival",
+    "to_local",
+)
 F32 = jnp.float32
 BF16 = jnp.bfloat16
 
@@ -71,65 +109,102 @@
     return jnp.where(rows == index, 1.0, 0.0).astype(BF16)
 
 
-def shift_level(high_ref, low_ref, fields, digits):
+def shift_level(high_ref, low_ref, fields, digits, operators):
     fh, fl = split(fields)
     total = jnp.zeros((KP, 128), F32)
-    for c in range(8):
-        mask = jnp.where(digits == c, 1.0, 0.0).astype(BF16)
-        ch, cl = fh * mask, fl * mask
-        total = total + (mm(high_ref[c], ch) + (mm(high_ref[c], cl) + mm(low_ref[c], ch)))
+    for at in range(0, len(operators), 2):
+        group = operators[at : at + 2]
+        masks = [jnp.where(digits == c, 1.0, 0.0).astype(BF16) for c in group]
+        high = jnp.concatenate([high_ref[c] for c in group], axis=1)
+        low = jnp.concatenate([low_ref[c] for c in group], axis=1)
+        bh = jnp.concatenate([fh * mask for mask in masks], axis=0)
+        bl = jnp.concatenate([fl * mask for mask in masks], axis=0)
+        both = mm(high, jnp.concatenate([bh, bl], axis=1))
+        total = total + (both[:, :128] + (both[:, 128:] + mm(low, bh)))
     return total
 
 
-def scatter_block(rows, target):
+def class_factors(table, klass):
+    width = klass.shape[1]
+    rows = lax.broadcasted_iota(jnp.int32, (128, width), 0)
+    return mm(table, jnp.where(rows % 64 == klass, 1.0, 0.0).astype(BF16))
+
+
+def halves(rows):
     hi, lo = split(rows)
+    return jnp.concatenate([hi, lo], axis=1)
+
+
+def scatter(target, pair):
     hot = one_hot_rows(target)
-    return mm_nt(jnp.concatenate([hi, lo], axis=1), jnp.concatenate([hot, hot], axis=1))
-
-
-def kernel(
-    comm,
-    multipole_ref,
-    local5_ref,
-    ids_ref,
-    count_ref,
-    up_ref,
-    down_ref,
-    lattice_ref,
-    to_wave_ref,
-    to_local_ref,
-    shift_ref,
-    near_source_ref,
-    near_target_ref,
-    near_class_ref,
-    far_source_ref,
-    far_class_ref,
-    far_count_ref,
-    arrival_ref,
-    out_ref,
-    moments,
-    far_moments,
-    pack,
-    far_pack,
-    padded,
-    up_high,
-    up_low,
-    down_high,
-    down_low,
-    expansion,
-    factor,
-    sums,
-    ring_a,
-    ring_b,
-    far_send,
-    far_recv,
-    pack_send,
-    pack_recv,
-    a_send,
-    a_recv,
-    b_send,
-    b_recv,
-):
+    return mm_nt(jnp.concatenate([hot, hot], axis=1), pair)
+
+
+def kernel(comm, *refs):
+    given, out_ref, held, rest = refs[:17], refs[17], refs[18:35], refs[35:]
+    (
+        multipole_ref,
+        local5_ref,
+        ids_ref,
+        count_ref,
+        up_ref,
+        down_ref,
+        lattice_ref,
+        to_wave_ref,
+        to_local_ref,
+        shift_ref,
+        near_source_ref,
+        near_target_ref,
+        near_class_ref,
+        far_source_ref,
+        far_class_ref,
+        far_count_ref,
+        arrival_ref,
+    ) = held
+    (
+        load_sem,
+        moments,
+        far_moments,
+        pack,
+        far_pack,
+        padded,
+        up_high,
+        up_low,
+        down_high,
+        down_low,
+        expansion,
+        wide,
+        wave_halves,
+        held_rows,
+        table_rows,
+        factor,
+        sums,
+        ring_a,
+        ring_b,
+        far_send,
+        far_recv,
+        pack_send,
+        pack_recv,
+        a_send,
+        a_recv,
+        b_send,
+        b_recv,
+    ) = rest
+    loads = {
+        name: pltpu.make_async_copy(
+            given[i],
+            held[i].at[pl.ds(0, 8 * K)] if name in ("up", "down") else held[i],
+            load_sem.at[i],
+        )
+        for i, name in enumerate(LOADS)
+    }
+    for name in LOAD_ORDER:
+        loads[name].start()
+
+    def loaded(*names):
+        for name in names:
+            loads[name].wait()
+
     if comm:
         octant, box = lax.axis_index("oct"), lax.axis_index("box")
         flat = octant * 32 + box
@@ -159,6 +234,7 @@
 
         lax.fori_loop(1, 16, greet, 0)
 
+    loaded("count", "multipole")
     lanes = lane_iota(1)
     count = count_ref[0]
     valid = jnp.where(lanes < 8 * count, 1.0, 0.0)
@@ -166,6 +242,7 @@
     moments[...] = jnp.zeros((KP, 128), F32)
     moments[:K, :] = multipole_ref[...] * valid
 
+    loaded("far_count", "far_source", "far_class")
     wide_lane = lax.broadcasted_iota(jnp.int32, (NEIGH, CAP), 1)
     row_number = lax.broadcasted_iota(jnp.int32, (NEIGH, CAP), 0)
     for d in range(DIRS):
@@ -175,22 +252,30 @@
         source = jnp.where(wide_lane < limit, far_source_ref[d], -1)
         pack[:, d, :] = jnp.concatenate([source, far_class_ref[d]], axis=1)
 
+    loaded("up", "down")
+    for ref in (up_ref, down_ref):
+        ref[8 * K :, :] = jnp.zeros((8 * (KP - K), K), F32)
     padded[...] = jnp.zeros((KP, KP), F32)
     for c in range(8):
-        padded[:K, :K] = up_ref[:, c, :]
+        padded[:, :K] = up_ref[pl.ds(c, KP, stride=8), :]
         up_high[c], up_low[c] = split(padded[...])
-        padded[:K, :K] = down_ref[:, c, :]
+        padded[:, :K] = down_ref[pl.ds(c, KP, stride=8), :]
         down_high[c], down_low[c] = split(padded[...])
 
-    ids = jnp.concatenate([ids_ref[...], jnp.zeros((1, 128 - BOX5), jnp.int32)], axis=1)
-    parent_of = lane_iota(8) // 8
-    ids = pick_lanes(jnp.broadcast_to(ids, (8, 128)), parent_of[:1])[:1]
+    loaded("ids")
+    first = ids_ref[0]
+    parent_of = lanes // 8
     child = lanes % 8
+    ids = first + parent_of
     digit = [(ids >> (3 * (DEPTH - j))) & 7 for j in range(1, DEPTH + 1)]
-
-    upward = shift_level(up_high, up_low, moments[...], child)
+    chosen = [
+        [((first >> (3 * (DEPTH - j))) + i) & 7 for i in range(2 if j < DEPTH - 1 else 3)]
+        for j in range(1, DEPTH)
+    ] + [list(range(8))]
+
+    upward = shift_level(up_high, up_low, moments[...], child, range(8))
     for j in range(DEPTH - 1, -1, -1):
-        upward = shift_level(up_high, up_low, upward, digit[j])
+        upward = shift_level(up_high, up_low, upward, digit[j], chosen[j])
     upward = upward * valid
     ring_a[0] = jnp.sum(jnp.transpose(upward), axis=0, keepdims=True)
 
@@ -247,24 +332,46 @@
             far_moments[n] = moments[...]
             far_pack[n] = pack[n]
 
-    def near_direction(d, carry):
-        weight = to_wave_ref[d]
-        mh, ml = split(moments[:K, :])
-        wh, wl = split(weight)
-        expansion[...] = mm(wh, mh) + (mm(wh, ml) + mm(wl, mh))
-        table = jnp.concatenate([shift_ref[d], jnp.zeros((128 - CLASSES, NEXP), F32)], axis=0)
-        factor[d] = jnp.transpose(table)
-        total = jnp.zeros((NEXP, 128), F32)
-        for block in range(BLOCKS):
-            source = near_source_ref[d, pl.ds(block, 1), :]
-            klass = near_class_ref[d, pl.ds(block, 1), :]
-            target = near_target_ref[d, pl.ds(block, 1), :]
-            rows = pick_lanes(expansion[...], source) * pick_lanes(factor[d], klass)
-            total = total + scatter_block(rows, target)
-        sums[d] = total
+    loaded("to_wave", "shift", "near_source", "near_class", "near_target")
+    table_rows[...] = jnp.zeros((128, NEXP), F32)
+    wide[...] = jnp.zeros((NEXP, KP), F32)
+    mh, ml = split(moments[...])
+    for d in range(DIRS):
+        wide[:, :K] = to_wave_ref[d]
+        wh, wl = split(wide[...])
+        wave_halves[d] = jnp.concatenate([wh, wl], axis=1)
+        both = mm(wh, jnp.concatenate([mh, ml], axis=1))
+        expansion[d] = both[:, :128] + (both[:, 128:] + mm(wl, mh))
+        high, low = split(shift_ref[d])
+        table_rows[:CLASSES, :] = high.astype(F32)
+        table_rows[64 : 64 + CLASSES, :] = low.astype(F32)
+        factor[d] = jnp.transpose(table_rows[...]).astype(BF16)
+
+    def near_rows(d, block):
+        klass = [near_class_ref[d, pl.ds(block + i, 1), :] for i in range(2)]
+        factors = class_factors(factor[d], jnp.concatenate(klass, axis=1))
+        for i in range(2):
+            source = near_source_ref[d, pl.ds(block + i, 1), :]
+            rows = pick_lanes(expansion[d], source) * factors[:, 128 * i : 128 * (i + 1)]
+            held_rows[block + i] = halves(rows)
+
+    def near_sums(d, block):
+        return scatter(near_target_ref[d, pl.ds(block, 1), :], held_rows[block]) + scatter(
+            near_target_ref[d, pl.ds(block + 1, 1), :], held_rows[block + 1]
+        )
+
+    def near_step(d, carry):
+        total = jnp.zeros((128, NEXP), F32)
+        for block in range(0, BLOCKS, 2):
+            total = total + near_sums(d - 1, block)
+            near_rows(d, block)
+        sums[d - 1] = total
         return carry
 
-    lax.fori_loop(0, DIRS // 2, near_direction, 0)
+    for block in range(0, BLOCKS, 2):
+        near_rows(0, block)
+
+    lax.fori_loop(1, 3, near_step, 0)
 
     if comm:
         for_peers(lambda k: copy_a(k).wait())
@@ -273,7 +380,7 @@
     else:
         ring_b[0] = ring_a[0]
 
-    lax.fori_loop(DIRS // 2, DIRS, near_direction, 0)
+    lax.fori_loop(3, 5, near_step, 0)
 
     if comm:
         for_peers(lambda k: copy_b(k).wait())
@@ -281,48 +388,68 @@
     else:
         root = ring_b[0]
 
+    near_step(DIRS - 1, 0)
+    total = jnp.zeros((128, NEXP), F32)
+    for block in range(0, BLOCKS, 2):
+        total = total + near_sums(DIRS - 1, block)
+    sums[DIRS - 1] = total
+
+    loaded("lattice", "local5", "arrival", "to_local")
     padded[:K, :K] = lattice_ref[...]
     ah, al = split(padded[...])
     rh, rl = split(jnp.broadcast_to(root, (128, KP)))
     downward = mm_nt(ah, rh) + (mm_nt(ah, rl) + mm_nt(al, rh))
     for j in range(DEPTH):
-        downward = shift_level(down_high, down_low, downward, digit[j])
+        downward = shift_level(down_high, down_low, downward, digit[j], chosen[j])
     padded[...] = jnp.zeros((KP, KP), F32)
     padded[:BOX5, :K] = local5_ref[...]
-    coarse = pick_lanes(jnp.transpose(padded[...]), parent_of[:1]) + downward
-    result = shift_level(down_high, down_low, coarse, child)[:K]
-
-    if comm:
-        for pair in far:
-            for copy in pair:
-                copy.wait()
+    coarse = pick_lanes(jnp.transpose(padded[...]), parent_of) + downward
+    result = shift_level(down_high, down_low, coarse, child, range(8))[:K]
 
     first_half = lanes < CAP
 
-    def far_direction(d, result):
-        wh, wl = split(to_wave_ref[d])
-        total = sums[d]
-        arrival = jnp.concatenate([arrival_ref[d], arrival_ref[d]], axis=1)
-        for p in range(NEIGH // 2):
-            one = far_pack[2 * p, pl.ds(d, 1), :]
-            two = far_pack[2 * p + 1, pl.ds(d, 1), :]
-            source = jnp.where(first_half, one, pltpu.roll(two, CAP, 1))
-            klass = jnp.where(first_half, pltpu.roll(one, CAP, 1), two)
-            target = jnp.where(first_half, arrival[2 * p : 2 * p + 1], arrival[2 * p + 1 : 2 * p + 2])
-            target = jnp.where(source >= 0, target, -1)
-            source = jnp.maximum(source, 0)
-            picked = jnp.where(
-                first_half,
-                pick_lanes(far_moments[2 * p], source),
-                pick_lanes(far_moments[2 * p + 1], source),
-            )[:K]
-            ph, pl_ = split(picked)
-            rows = mm(wh, ph) + (mm(wh, pl_) + mm(wl, ph))
-            rows = rows * pick_lanes(factor[d], klass)
-            total = total + scatter_block(rows, target)
-        return result + mm3(to_local_ref[d], total)
-
-    result = lax.fori_loop(0, DIRS, far_direction, result)
+    def far_blocks(group):
+        for d in range(DIRS):
+            sources, klasses, targets, picked = [], [], [], []
+            arrival = jnp.concatenate([arrival_ref[d], arrival_ref[d]], axis=1)
+            for p in (2 * group, 2 * group + 1):
+                one = far_pack[2 * p, d : d + 1, :]
+                two = far_pack[2 * p + 1, d : d + 1, :]
+                source = jnp.where(first_half, one, pltpu.roll(two, CAP, 1))
+                klasses.append(jnp.where(first_half, pltpu.roll(one, CAP, 1), two))
+                target = jnp.where(
+                    first_half, arrival[2 * p : 2 * p + 1], arrival[2 * p + 1 : 2 * p + 2]
+                )
+                targets.append(jnp.where(source >= 0, target, -1))
+                source = jnp.maximum(source, 0)
+                picked.append(
+                    jnp.where(
+                        first_half,
+                        pick_lanes(far_moments[2 * p], source),
+                        pick_lanes(far_moments[2 * p + 1], source),
+                    )
+                )
+            ph, pl_ = split(jnp.concatenate(picked, axis=1))
+            both = wave_halves[d]
+            rows = mm(both, jnp.concatenate([ph, ph], axis=0)) + mm(both[:, :KP], pl_)
+            rows = rows * class_factors(factor[d], jnp.concatenate(klasses, axis=1))
+            total = sums[d]
+            for i in range(2):
+                total = total + scatter(targets[i], halves(rows[:, 128 * i : 128 * (i + 1)]))
+            sums[d] = total
+
+    for group in range(2):
+        if comm:
+            for n in range(4 * group, 4 * group + 4):
+                for copy in far[n]:
+                    copy.wait()
+        far_blocks(group)
+
+    for d in range(DIRS):
+        vh, vl = split(to_local_ref[d])
+        th, tl = split(sums[d])
+        both = mm_nt(vh, jnp.concatenate([th, tl], axis=0))
+        result = result + (both[:, :128] + (both[:, 128:] + mm_nt(vl, th)))
     out_ref[...] = result * valid
 
 
@@ -346,15 +473,38 @@
     arrival_slot,
     comm=True,
 ):
-    vmem = pl.BlockSpec(memory_space=pltpu.VMEM)
-    smem = pl.BlockSpec(memory_space=pltpu.SMEM)
     dma = pltpu.SemaphoreType.DMA
+    operands = (
+        multipole6,
+        jnp.transpose(local5),
+        box_ids,
+        box_count,
+        jnp.transpose(up_shift, (1, 0, 2)).reshape(8 * K, K),
+        jnp.transpose(down_shift, (1, 0, 2)).reshape(8 * K, K),
+        periodic_lattice_operator,
+        multipole_to_wave_maps,
+        wave_to_local_maps,
+        wave_shift,
+        local_source.reshape(DIRS, BLOCKS, 128),
+        local_target.reshape(DIRS, BLOCKS, 128),
+        local_class.reshape(DIRS, BLOCKS, 128),
+        remote_source.reshape(DIRS, NEIGH, CAP),
+        remote_class.reshape(DIRS, NEIGH, CAP),
+        remote_count,
+        arrival_slot.reshape(DIRS, NEIGH, CAP),
+    )
+    held = []
+    for name, value in zip(LOADS, operands):
+        space = pltpu.SMEM if name in ("ids", "count", "far_count") else pltpu.VMEM
+        shape = (8 * KP, K) if name in ("up", "down") else value.shape
+        held.append(space(shape, value.dtype))
     return pl.pallas_call(
         functools.partial(kernel, comm),
         out_shape=jax.ShapeDtypeStruct((K, SLOTS), F32),
-        in_specs=[vmem] * 3 + [smem] + [vmem] * 11 + [smem] + [vmem],
-        out_specs=vmem,
-        scratch_shapes=[
+        in_specs=[pl.BlockSpec(memory_space=pltpu.HBM)] * len(operands),
+        out_specs=pl.BlockSpec(memory_space=pltpu.VMEM),
+        scratch_shapes=held + [
+            dma((len(operands),)),
             pltpu.VMEM((KP, 128), F32),
             pltpu.VMEM((NEIGH, KP, 128), F32),
             pltpu.VMEM((NEIGH, 8, 128), jnp.int32),
@@ -364,9 +514,13 @@
             pltpu.VMEM((8, KP, KP), BF16),
             pltpu.VMEM((8, KP, KP), BF16),
             pltpu.VMEM((8, KP, KP), BF16),
-            pltpu.VMEM((NEXP, 128), F32),
             pltpu.VMEM((DIRS, NEXP, 128), F32),
-            pltpu.VMEM((DIRS, NEXP, 128), F32),
+            pltpu.VMEM((NEXP, KP), F32),
+            pltpu.VMEM((DIRS, NEXP, 2 * KP), BF16),
+            pltpu.VMEM((BLOCKS, NEXP, 256), BF16),
+            pltpu.VMEM((128, NEXP), F32),
+            pltpu.VMEM((DIRS, NEXP, 128), BF16),
+            pltpu.VMEM((DIRS, 128, NEXP), F32),
             pltpu.VMEM((16, 1, 128), F32),
             pltpu.VMEM((16, 1, 128), F32),
             dma((NEIGH,)),
@@ -379,29 +533,11 @@
             dma((15,)),
         ],
         compiler_params=pltpu.CompilerParams(
-            vmem_limit_bytes=40 * 1024 * 1024,
+            vmem_limit_bytes=60 * 1024 * 1024,
             **(dict(collective_id=0, has_side_effects=True) if comm else {}),
         ),
         name="downward_pass",
-    )(
-        multipole6,
-        jnp.transpose(local5),
-        box_ids.reshape(1, BOX5),
-        box_count,
-        jnp.transpose(up_shift, (1, 0, 2)),
-        jnp.transpose(down_shift, (1, 0, 2)),
-        periodic_lattice_operator,
-        multipole_to_wave_maps,
-        wave_to_local_maps,
-        wave_shift,
-        local_source.reshape(DIRS, BLOCKS, 128),
-        local_target.reshape(DIRS, BLOCKS, 128),
-        local_class.reshape(DIRS, BLOCKS, 128),
-        remote_source.reshape(DIRS, NEIGH, CAP),
-        remote_class.reshape(DIRS, NEIGH, CAP),
-        remote_count,
-        arrival_slot.reshape(DIRS, NEIGH, CAP),
-    )
+    )(*operands)
 
 
 def solution(mesh):

time: 50.7 us -> 34 us (0.67)
  local copies, waits for them, and re-layouts: 12.9 us -> 1.47 us
  Pallas kernels: 36.4 us -> 31.6 us
    unnamed x33 -> x1, local copies, waits for them, and re-layouts: 12.9 us -> 1.47 us
    pallas_call x1, Pallas kernels: 36.4 us -> 31.6 us  [local(): pl.pallas_call(functools.partial(kernel, comm), out_shape=jax.ShapeDtypeS...]
where the time goes in v1:
time: 34 us; the launch traced here: 33.7 us
  Pallas kernels  31.6 us (93%)
  local copies, waits for them, and re-layouts  1.47 us (4%)
  between operations  0.66 us (2%)
    pallas_call x1, Pallas kernels, local(): pl.pallas_call(functools.partial(kernel, comm), out_shape=jax.ShapeDtypeS...  31.6 us
    unnamed x1, local copies, waits for them, and re-layouts  1.47 us

profile of v1, /device:TPU:33, one launch (start us, length us, event | category | flops | bytes accessed | tf_op | source)
XLA Modules:
  0.0 33.7 jit_solution(15151956344860103047)
XLA Ops:
  0.7 31.6 %downward_pass.1 = f32[121,128]{1,0:T(8,128)} custom-call(f32[121,128]{1,0:T(8,128)} %refs_0_.1, f32[16,121]{1,0:T(8,128)} %bitcast.21, s32[16]{0:T(128)} %refs_2_.1, s32[1]{0:T(128)S(6)} %copy.19.refs_3_, f32[968,121]{1,0:T(8,128)} %bitcast.13, f32[968,121]{1,0:T(8,128)} %bitcast.14, f32[121,121]{1,0:T(8,128)} %refs_6_.1, f32[6,256,121]{2,1,0:T(8,128)} %refs_7_.1, ...), custom_call_target="tpu_custom_call" | custom-call | tf_op jit(solution)/shard_map/downward_pass/pallas_call | solution.py:501
  32.3 1.5 %copy.20 = f32[121,128]{1,0:T(8,128)} copy(f32[121,128]{1,0:T(8,128)} %downward_pass.1) | data formatting | bytes 123904

commit v2 on v1

--- a/solution.py
+++ b/solution.py
@@ -252,45 +252,19 @@
         source = jnp.where(wide_lane < limit, far_source_ref[d], -1)
         pack[:, d, :] = jnp.concatenate([source, far_class_ref[d]], axis=1)
 
-    loaded("up", "down")
-    for ref in (up_ref, down_ref):
-        ref[8 * K :, :] = jnp.zeros((8 * (KP - K), K), F32)
-    padded[...] = jnp.zeros((KP, KP), F32)
-    for c in range(8):
-        padded[:, :K] = up_ref[pl.ds(c, KP, stride=8), :]
-        up_high[c], up_low[c] = split(padded[...])
-        padded[:, :K] = down_ref[pl.ds(c, KP, stride=8), :]
-        down_high[c], down_low[c] = split(padded[...])
-
-    loaded("ids")
-    first = ids_ref[0]
-    parent_of = lanes // 8
-    child = lanes % 8
-    ids = first + parent_of
-    digit = [(ids >> (3 * (DEPTH - j))) & 7 for j in range(1, DEPTH + 1)]
-    chosen = [
-        [((first >> (3 * (DEPTH - j))) + i) & 7 for i in range(2 if j < DEPTH - 1 else 3)]
-        for j in range(1, DEPTH)
-    ] + [list(range(8))]
-
-    upward = shift_level(up_high, up_low, moments[...], child, range(8))
-    for j in range(DEPTH - 1, -1, -1):
-        upward = shift_level(up_high, up_low, upward, digit[j], chosen[j])
-    upward = upward * valid
-    ring_a[0] = jnp.sum(jnp.transpose(upward), axis=0, keepdims=True)
-
     if comm:
         pl.semaphore_wait(barrier, NEIGH + 15 + 15)
 
         def far_copies(n):
             who = neighbour(OFFSETS[n])
+            near_by = who if n < 4 else neighbour(OFFSETS[n - 4])
             return (
                 pltpu.make_async_remote_copy(
-                    src_ref=moments,
+                    src_ref=moments if n < 4 else far_moments.at[2 + n % 2],
                     dst_ref=far_moments.at[n],
                     send_sem=far_send.at[n],
                     recv_sem=far_recv.at[n],
-                    device_id=who,
+                    device_id=near_by,
                     device_id_type=MESH,
                 ),
                 pltpu.make_async_remote_copy(
@@ -322,17 +296,42 @@
 
         copy_a = lambda k: sum_copy(k, ring_a, a_send, a_recv, peer_a)
         copy_b = lambda k: sum_copy(k, ring_b, b_send, b_recv, peer_b)
-        for_peers(lambda k: copy_a(k).start())
         far = [far_copies(n) for n in range(NEIGH)]
-        for pair in far:
-            for copy in pair:
-                copy.start()
+        for n in range(4):
+            far[n][0].start()
+        for n in range(NEIGH):
+            far[n][1].start()
     else:
         for n in range(NEIGH):
             far_moments[n] = moments[...]
             far_pack[n] = pack[n]
 
-    loaded("to_wave", "shift", "near_source", "near_class", "near_target")
+    loaded("up", "down", "ids", "to_wave", "shift", "near_source", "near_class", "near_target")
+    for ref in (up_ref, down_ref):
+        ref[8 * K :, :] = jnp.zeros((8 * (KP - K), K), F32)
+    padded[...] = jnp.zeros((KP, KP), F32)
+    for c in range(8):
+        padded[:, :K] = up_ref[pl.ds(c, KP, stride=8), :]
+        up_high[c], up_low[c] = split(padded[...])
+        padded[:, :K] = down_ref[pl.ds(c, KP, stride=8), :]
+        down_high[c], down_low[c] = split(padded[...])
+
+    first = ids_ref[0]
+    parent_of = lanes // 8
+    child = lanes % 8
+    ids = first + parent_of
+    digit = [(ids >> (3 * (DEPTH - j))) & 7 for j in range(1, DEPTH + 1)]
+    chosen = [
+        [((first >> (3 * (DEPTH - j))) + i) & 7 for i in range(2 if j < DEPTH - 1 else 3)]
+        for j in range(1, DEPTH)
+    ] + [list(range(8))]
+
+    upward = shift_level(up_high, up_low, moments[...], child, range(8))
+    for j in range(DEPTH - 1, -1, -1):
+        upward = shift_level(up_high, up_low, upward, digit[j], chosen[j])
+    upward = upward * valid
+    ring_a[0] = jnp.sum(jnp.transpose(upward), axis=0, keepdims=True)
+
     table_rows[...] = jnp.zeros((128, NEXP), F32)
     wide[...] = jnp.zeros((NEXP, KP), F32)
     mh, ml = split(moments[...])
@@ -371,9 +370,16 @@
     for block in range(0, BLOCKS, 2):
         near_rows(0, block)
 
+    if comm:
+        for_peers(lambda k: copy_a(k).start())
+
     lax.fori_loop(1, 3, near_step, 0)
 
     if comm:
+        for n in (2, 3):
+            far[n][0].wait()
+        for n in range(4, NEIGH):
+            far[n][0].start()
         for_peers(lambda k: copy_a(k).wait())
         ring_b[0] = jnp.sum(ring_a[...], axis=0)
         for_peers(lambda k: copy_b(k).start())
@@ -387,12 +393,6 @@
         root = jnp.sum(ring_b[...], axis=0)
     else:
         root = ring_b[0]
-
-    near_step(DIRS - 1, 0)
-    total = jnp.zeros((128, NEXP), F32)
-    for block in range(0, BLOCKS, 2):
-        total = total + near_sums(DIRS - 1, block)
-    sums[DIRS - 1] = total
 
     loaded("lattice", "local5", "arrival", "to_local")
     padded[:K, :K] = lattice_ref[...]
@@ -405,6 +405,12 @@
     padded[:BOX5, :K] = local5_ref[...]
     coarse = pick_lanes(jnp.transpose(padded[...]), parent_of) + downward
     result = shift_level(down_high, down_low, coarse, child, range(8))[:K]
+
+    near_step(DIRS - 1, 0)
+    total = jnp.zeros((128, NEXP), F32)
+    for block in range(0, BLOCKS, 2):
+        total = total + near_sums(DIRS - 1, block)
+    sums[DIRS - 1] = total
 
     first_half = lanes < CAP
 
@@ -441,8 +447,9 @@
     for group in range(2):
         if comm:
             for n in range(4 * group, 4 * group + 4):
-                for copy in far[n]:
-                    copy.wait()
+                if n not in (2, 3):
+                    far[n][0].wait()
+                far[n][1].wait()
         far_blocks(group)
 
     for d in range(DIRS):

time: 34 us -> 34.8 us (1.024)
  the two profiles are of different devices: /device:TPU:33 before, /device:TPU:1 now
where the time goes in v2:
time: 34.8 us; the launch traced here: 34.6 us
  Pallas kernels  32.5 us (93%)
  local copies, waits for them, and re-layouts  1.47 us (4%)
  between operations  0.66 us (2%)
    pallas_call x1, Pallas kernels, local(): pl.pallas_call(functools.partial(kernel, comm), out_shape=jax.ShapeDtypeS...  32.5 us
    unnamed x1, local copies, waits for them, and re-layouts  1.47 us

profile of v2, /device:TPU:1, one launch (start us, length us, event | category | flops | bytes accessed | tf_op | source)
XLA Modules:
  0.0 34.6 jit_solution(12698400673814826807)
XLA Ops:
  0.7 32.5 %downward_pass.1 = f32[121,128]{1,0:T(8,128)} custom-call(f32[121,128]{1,0:T(8,128)} %refs_0_.1, f32[16,121]{1,0:T(8,128)} %bitcast.21, s32[16]{0:T(128)} %refs_2_.1, s32[1]{0:T(128)S(6)} %copy.19.refs_3_, f32[968,121]{1,0:T(8,128)} %bitcast.13, f32[968,121]{1,0:T(8,128)} %bitcast.14, f32[121,121]{1,0:T(8,128)} %refs_6_.1, f32[6,256,121]{2,1,0:T(8,128)} %refs_7_.1, ...), custom_call_target="tpu_custom_call" | custom-call | tf_op jit(solution)/shard_map/downward_pass/pallas_call | solution.py:508
  33.2 1.5 %copy.20 = f32[121,128]{1,0:T(8,128)} copy(f32[121,128]{1,0:T(8,128)} %downward_pass.1) | data formatting | bytes 123904

commit v3 on v2

--- a/solution.py
+++ b/solution.py
@@ -205,6 +205,8 @@
         for name in names:
             loads[name].wait()
 
+    far_moments[:, K:, :] = jnp.zeros((NEIGH, KP - K, 128), F32)
+
     if comm:
         octant, box = lax.axis_index("oct"), lax.axis_index("box")
         flat = octant * 32 + box
@@ -257,11 +259,12 @@
 
         def far_copies(n):
             who = neighbour(OFFSETS[n])
-            near_by = who if n < 4 else neighbour(OFFSETS[n - 4])
+            relayed = n % 4 >= 2
+            near_by = neighbour(OFFSETS[n % 2]) if relayed else who
             return (
                 pltpu.make_async_remote_copy(
-                    src_ref=moments if n < 4 else far_moments.at[2 + n % 2],
-                    dst_ref=far_moments.at[n],
+                    src_ref=(far_moments.at[n - 2] if relayed else moments).at[pl.ds(0, K)],
+                    dst_ref=far_moments.at[n, pl.ds(0, K)],
                     send_sem=far_send.at[n],
                     recv_sem=far_recv.at[n],
                     device_id=near_by,
@@ -297,7 +300,7 @@
         copy_a = lambda k: sum_copy(k, ring_a, a_send, a_recv, peer_a)
         copy_b = lambda k: sum_copy(k, ring_b, b_send, b_recv, peer_b)
         far = [far_copies(n) for n in range(NEIGH)]
-        for n in range(4):
+        for n in (4, 5, 0, 1):
             far[n][0].start()
         for n in range(NEIGH):
             far[n][1].start()
@@ -306,15 +309,16 @@
             far_moments[n] = moments[...]
             far_pack[n] = pack[n]
 
-    loaded("up", "down", "ids", "to_wave", "shift", "near_source", "near_class", "near_target")
-    for ref in (up_ref, down_ref):
-        ref[8 * K :, :] = jnp.zeros((8 * (KP - K), K), F32)
+    loaded("up", "ids")
     padded[...] = jnp.zeros((KP, KP), F32)
-    for c in range(8):
-        padded[:, :K] = up_ref[pl.ds(c, KP, stride=8), :]
-        up_high[c], up_low[c] = split(padded[...])
-        padded[:, :K] = down_ref[pl.ds(c, KP, stride=8), :]
-        down_high[c], down_low[c] = split(padded[...])
+
+    def halve_operators(operators_ref, high_ref, low_ref):
+        operators_ref[8 * K :, :] = jnp.zeros((8 * (KP - K), K), F32)
+        for c in range(8):
+            padded[:, :K] = operators_ref[pl.ds(c, KP, stride=8), :]
+            high_ref[c], low_ref[c] = split(padded[...])
+
+    halve_operators(up_ref, up_high, up_low)
 
     first = ids_ref[0]
     parent_of = lanes // 8
@@ -331,6 +335,9 @@
         upward = shift_level(up_high, up_low, upward, digit[j], chosen[j])
     upward = upward * valid
     ring_a[0] = jnp.sum(jnp.transpose(upward), axis=0, keepdims=True)
+    if comm:
+        for_peers(lambda k: copy_a(k).start())
+    loaded("to_wave", "shift", "near_source", "near_class", "near_target")
 
     table_rows[...] = jnp.zeros((128, NEXP), F32)
     wide[...] = jnp.zeros((NEXP, KP), F32)
@@ -370,47 +377,31 @@
     for block in range(0, BLOCKS, 2):
         near_rows(0, block)
 
-    if comm:
-        for_peers(lambda k: copy_a(k).start())
-
-    lax.fori_loop(1, 3, near_step, 0)
-
-    if comm:
-        for n in (2, 3):
+
+    def hand_on(*slots):
+        for n in slots:
             far[n][0].wait()
-        for n in range(4, NEIGH):
-            far[n][0].start()
+            far[n + 2][0].start()
+
+    lax.fori_loop(1, 4, near_step, 0)
+    if comm:
+        hand_on(0, 1)
+    lax.fori_loop(4, 5, near_step, 0)
+    if comm:
+        hand_on(4, 5)
         for_peers(lambda k: copy_a(k).wait())
         ring_b[0] = jnp.sum(ring_a[...], axis=0)
         for_peers(lambda k: copy_b(k).start())
     else:
         ring_b[0] = ring_a[0]
 
-    lax.fori_loop(3, 5, near_step, 0)
-
-    if comm:
-        for_peers(lambda k: copy_b(k).wait())
-        root = jnp.sum(ring_b[...], axis=0)
-    else:
-        root = ring_b[0]
-
-    loaded("lattice", "local5", "arrival", "to_local")
-    padded[:K, :K] = lattice_ref[...]
-    ah, al = split(padded[...])
-    rh, rl = split(jnp.broadcast_to(root, (128, KP)))
-    downward = mm_nt(ah, rh) + (mm_nt(ah, rl) + mm_nt(al, rh))
-    for j in range(DEPTH):
-        downward = shift_level(down_high, down_low, downward, digit[j], chosen[j])
-    padded[...] = jnp.zeros((KP, KP), F32)
-    padded[:BOX5, :K] = local5_ref[...]
-    coarse = pick_lanes(jnp.transpose(padded[...]), parent_of) + downward
-    result = shift_level(down_high, down_low, coarse, child, range(8))[:K]
-
+    loaded("down", "lattice", "local5", "arrival", "to_local")
     near_step(DIRS - 1, 0)
     total = jnp.zeros((128, NEXP), F32)
     for block in range(0, BLOCKS, 2):
         total = total + near_sums(DIRS - 1, block)
     sums[DIRS - 1] = total
+    halve_operators(down_ref, down_high, down_low)
 
     first_half = lanes < CAP
 
@@ -418,7 +409,7 @@
         for d in range(DIRS):
             sources, klasses, targets, picked = [], [], [], []
             arrival = jnp.concatenate([arrival_ref[d], arrival_ref[d]], axis=1)
-            for p in (2 * group, 2 * group + 1):
+            for p in (group, group + 2):
                 one = far_pack[2 * p, d : d + 1, :]
                 two = far_pack[2 * p + 1, d : d + 1, :]
                 source = jnp.where(first_half, one, pltpu.roll(two, CAP, 1))
@@ -444,20 +435,37 @@
                 total = total + scatter(targets[i], halves(rows[:, 128 * i : 128 * (i + 1)]))
             sums[d] = total
 
-    for group in range(2):
-        if comm:
-            for n in range(4 * group, 4 * group + 4):
-                if n not in (2, 3):
-                    far[n][0].wait()
-                far[n][1].wait()
-        far_blocks(group)
-
+    if comm:
+        for n in (0, 1, 4, 5):
+            far[n][1].wait()
+    far_blocks(0)
+
+    if comm:
+        for_peers(lambda k: copy_b(k).wait())
+        root = jnp.sum(ring_b[...], axis=0)
+        for n in (2, 3, 6, 7):
+            far[n][0].wait()
+            far[n][1].wait()
+    else:
+        root = ring_b[0]
+    padded[:K, :K] = lattice_ref[...]
+    ah, al = split(padded[...])
+    rh, rl = split(jnp.broadcast_to(root, (128, KP)))
+    downward = mm_nt(ah, rh) + (mm_nt(ah, rl) + mm_nt(al, rh))
+    for j in range(DEPTH):
+        downward = shift_level(down_high, down_low, downward, digit[j], chosen[j])
+    padded[...] = jnp.zeros((KP, KP), F32)
+    padded[:BOX5, :K] = local5_ref[...]
+    coarse = pick_lanes(jnp.transpose(padded[...]), parent_of) + downward
+    result = shift_level(down_high, down_low, coarse, child, range(8))[:K]
+
+    far_blocks(1)
     for d in range(DIRS):
         vh, vl = split(to_local_ref[d])
         th, tl = split(sums[d])
         both = mm_nt(vh, jnp.concatenate([th, tl], axis=0))
         result = result + (both[:, :128] + (both[:, 128:] + mm_nt(vl, th)))
-    out_ref[...] = result * valid
+    out_ref[...] = result
 
 
 def local(
@@ -505,7 +513,7 @@
         space = pltpu.SMEM if name in ("ids", "count", "far_count") else pltpu.VMEM
         shape = (8 * KP, K) if name in ("up", "down") else value.shape
         held.append(space(shape, value.dtype))
-    return pl.pallas_call(
+    result = pl.pallas_call(
         functools.partial(kernel, comm),
         out_shape=jax.ShapeDtypeStruct((K, SLOTS), F32),
         in_specs=[pl.BlockSpec(memory_space=pltpu.HBM)] * len(operands),
@@ -545,6 +553,7 @@
         ),
         name="downward_pass",
     )(*operands)
+    return result * (jnp.arange(SLOTS, dtype=jnp.int32) < 8 * box_count).astype(F32)[None, :]
 
 
 def solution(mesh):

time: 34.8 us -> 33.5 us (0.963)
  the two profiles are of different devices: /device:TPU:1 before, /device:TPU:6 now
where the time goes in v3:
time: 33.5 us; the launch traced here: 33.4 us
  Pallas kernels  31.2 us (93%)
  other arithmetic  1.48 us (4%)
  between operations  0.67 us (2%)
    pallas_call x1, Pallas kernels, local(): pl.pallas_call(functools.partial(kernel, comm), out_shape=jax.ShapeDtypeS...  31.2 us
    mul x1, other arithmetic, local(): result * (jnp.arange(SLOTS, dtype=jnp.int32) < 8 * box_count).astype(F32)...  1.48 us

profile of v3, /device:TPU:6, one launch (start us, length us, event | category | flops | bytes accessed | tf_op | source)
XLA Modules:
  0.0 33.4 jit_solution(15907023532315472932)
XLA Ops:
  0.7 31.2 %downward_pass.1 = f32[121,128]{1,0:T(8,128)} custom-call(f32[121,128]{1,0:T(8,128)} %refs_0_.1, f32[16,121]{1,0:T(8,128)} %bitcast.22, s32[16]{0:T(128)} %refs_2_.1, s32[1]{0:T(128)S(6)} %copy.18.refs_3_, f32[968,121]{1,0:T(8,128)} %bitcast.14, f32[968,121]{1,0:T(8,128)} %bitcast.15, f32[121,121]{1,0:T(8,128)} %refs_6_.1, f32[6,256,121]{2,1,0:T(8,128)} %refs_7_.1, ...), custom_call_target="tpu_custom_call" | custom-call | tf_op jit(solution)/shard_map/downward_pass/pallas_call | solution.py:516
  31.9 1.5 %broadcast_multiply_fusion = f32[121,128]{1,0:T(8,128)} fusion(f32[121,128]{1,0:T(8,128)} %downward_pass.1, f32[128]{0:T(128)S(1)} %compare_convert_fusion), kind=kLoop, calls=%fused_computation | loop fusion | flops 15488 | bytes 124416 | tf_op jit(solution)/shard_map/mul | solution.py:556
  (1 shorter events, 0.0 us)
